TPU v7x, 1024 devices: a whole 4x8x16 slice. The times are simulated.
1024 devices in a mesh: row: 8 (over z_lo), col: 128 (over y, x, z_hi, core).
Axes of the slice: x: 4, y: 8, z: 16 (z_hi: 2, z_lo: 8; z = z_hi * 8 + z_lo), core: 2. Of those that a mesh axis runs over, the one named last changes fastest.
Arguments:
- kernel: bfloat16 [2, 2, 32768, 2048], P(None, None, 'col', 'row'), may hold values from -0.0234375 to 0.0234375
- probes: bfloat16 [256, 2, 2, 32768], P(None, None, None, 'col'), may hold values from -6 to 6
- noise_var: float32 [2, 32768], P(None, 'col'), may hold values from 0.05 to 0.5
- prior_diag: float32 [2048], P('row'), may hold values from 2.2 to 4
Outputs:
- hess_probes: float32 [256, 2, 2, 32768], P('row', None, None, 'col')
All inputs are finite; a program needn't handle non-finite values.
Results may differ from a plain program's by a relative error of at most 0.015.
Values may be sent and summed in bfloat16 or wider, within the bound.
A program may use at most 32 MiB of HBM per device.

v0:
```python
import jax
import jax.numpy as jnp
from jax import lax
from jax.sharding import PartitionSpec as P


def extended(block, sides, width):
    for axis, dim in sides:
        count = lax.axis_size(axis)
        forward = [(i, i + 1) for i in range(count - 1)]
        backward = [(target, source) for source, target in forward]
        low = lax.ppermute(
            lax.slice_in_dim(block, block.shape[dim] - width, None, axis=dim), axis, forward
        )
        high = lax.ppermute(lax.slice_in_dim(block, 0, width, axis=dim), axis, backward)
        block = jnp.concatenate([low, block, high], axis=dim)
    return block


def sweep(field, coef, below, above):
    return coef * field - below - above


def apply_prior(block, coef):
    shape = block.shape
    par_count = shape[-1]
    flat = block.reshape(-1, par_count)
    result = flat
    for sweep_no in range(2):
        wide = extended(result.astype(jnp.bfloat16), (("row", 1),), 1).astype(result.dtype)
        result = sweep(result, coef, wide[:, :-2], wide[:, 2:])
    return result.reshape(shape)


def shards(kernel, probes, noise_var, prior_diag):
    freq_count = kernel.shape[0]
    row_count = kernel.shape[2]
    par_count = kernel.shape[3]
    col_count = probes.shape[0]
    stacks = [kernel[freq_no].reshape(2 * row_count, par_count) for freq_no in range(freq_count)]
    adjoint = []
    for freq_no in range(freq_count):
        real_part = probes[:, freq_no, 0, :]
        imag_part = probes[:, freq_no, 1, :]
        upper = jnp.concatenate([real_part, imag_part], axis=1)
        lower = jnp.concatenate([imag_part, -real_part], axis=1)
        product = jnp.dot(
            jnp.concatenate([upper, lower], axis=0),
            stacks[freq_no],
            preferred_element_type=jnp.float32,
        )
        adjoint.append(product.reshape(2, col_count, par_count))
    adjoint = jnp.stack(adjoint)
    summed = lax.psum(adjoint, "col")
    field = apply_prior(summed, prior_diag).astype(jnp.bfloat16)
    rows_own = col_count // lax.axis_size("row")
    count = lax.axis_size("row") * rows_own
    parts = []
    for freq_no in range(freq_count):
        real_rows = field[freq_no, 0]
        imag_rows = field[freq_no, 1]
        both = jnp.concatenate([real_rows, imag_rows], axis=0)
        prod = lax.dot_general(
            both, stacks[freq_no], (((1,), (1,)), ((), ())), preferred_element_type=jnp.float32
        )
        real_out = prod[:count, :row_count] - prod[count:, row_count:]
        imag_out = prod[count:, :row_count] + prod[:count, row_count:]
        parts.append(jnp.stack([real_out, imag_out], axis=1))
    total = lax.psum_scatter(
        jnp.stack(parts, axis=1).astype(jnp.bfloat16), "row", scatter_dimension=0, tiled=True
    ).astype(jnp.float32)
    first_row = lax.axis_index("row") * rows_own
    own_probes = lax.dynamic_slice_in_dim(probes, first_row, rows_own, 0).astype(jnp.float32)
    return total + noise_var[None, :, None, :] * own_probes


def solution(mesh):
    in_specs = (P(None, None, "col", "row"), P(None, None, None, "col"), P(None, "col"), P("row"))
    out_specs = P("row", None, None, "col")
    return jax.shard_map(shards, mesh=mesh, in_specs=in_specs, out_specs=out_specs, check_vma=False)
```

profile of v0, /device:TPU:2, one launch (start us, length us, event | category | flops | bytes accessed | tf_op | source)
XLA Modules:
  0.0 2259.6 jit_solution(6132943794597987426)
XLA Ops:
  6.5 0.0 copy-start.1
  6.5 0.0 all-reduce.2.cloned.1.call-start
  6.5 2.2 fusion.25
  8.8 0.0 copy-done.1
  9.0 0.3 convolution_bitcast_fusion.1
  9.3 0.3 convolution_bitcast_fusion
  9.6 1.1 pad_maximum_fusion
  10.7 0.0 all-reduce.2.cloned.1.call-update
  10.7 0.0 reduce-scatter.2.cloned.1.call-start
  10.7 2137.9 %all-reduce.2.cloned.1.call-done = f32[1024,256]{1,0:T(8,128)} async-done(((f32[1024,256]{1,0:T(8,128)}), f32[1024,256]{1,0:T(8,128)}) %all-reduce.2.cloned.1.call-update) | async-done | bytes 1048592 | tf_op jit(solution)/shard_map/psum | solution.py:54
  2148.6 1.3 convert_element_type.25
  2149.9 0.1 fusion.23
  2150.1 0.0 copy-start
  2150.1 0.0 copy-start.2
  2150.1 2.2 collective-permute-start
  2152.3 1.3 collective-permute-start.1
  2153.6 4.3 collective-permute-done
  2157.9 4.1 collective-permute-done.1
  2162.0 0.4 maximum_convert_fusion
  2162.5 0.0 copy-done
  2162.5 0.0 copy-done.2
  2162.5 0.5 fusion.19
  2163.0 0.1 fusion.22
  2163.1 2.7 collective-permute-start.2
  2165.8 1.3 collective-permute-start.3
  2167.1 3.1 collective-permute-done.2
  2170.2 4.1 collective-permute-done.3
  2174.3 0.4 maximum_convert_fusion.1
  2174.8 0.7 fusion
  2175.6 0.3 fusion.5
  2175.9 0.1 fusion.13
  2176.0 0.3 fusion.9
  2176.3 0.1 fusion.15
  2176.3 0.0 copy-start.3
  2176.4 0.8 pad_maximum_fusion.1
  2177.3 0.0 reduce-scatter.2.cloned.1.call-update
  2177.3 0.9 constant_dynamic-slice_fusion
  2178.2 72.9 %reduce-scatter.2.cloned.1.call-done = bf16[32,2,2,256]{3,0,2,1:T(8,128)(2,1)} async-done(((bf16[256,2,2,256]{3,0,2,1:T(8,128)(2,1)}), bf16[32,2,2,256]{3,0,2,1:T(8,128)(2,1)}) %reduce-scatter.2.cloned.1.call-update) | async-done | bytes 65552 | tf_op jit(solution)/shard_map/reduce_scatter | solution.py:69
  2251.1 0.0 copy-done.3
  2251.1 0.9 multiply_add_fusion
  2252.0 0.8 copy.14
  (8 shorter events, 0.3 us)
Async XLA Ops:
  6.5 2.2 copy-start.1
  6.5 2142.1 %all-reduce.2.cloned.1.call-start = ((), (), s32[]{:S(2)}) async-start(), calls=%async_computation.1 | async-start | bytes 2097152 | tf_op jit(solution)/shard_map/psum | solution.py:54
  10.7 2240.4 %reduce-scatter.2.cloned.1.call-start = ((), (), s32[]{:S(2)}) async-start(), calls=%async_computation.2 | async-start | bytes 589824 | tf_op jit(solution)/shard_map/reduce_scatter | solution.py:69
  2150.1 12.4 copy-start
  2150.1 12.4 copy-start.2
  2150.1 7.8 collective-permute-start
  2152.3 9.8 collective-permute-start.1
  2163.1 7.1 collective-permute-start.2
  2165.8 8.6 collective-permute-start.3
  2176.3 74.8 %copy-start.3 = (f32[2,256]{1,0:T(2,128)S(1)}, f32[2,256]{1,0:T(2,128)}, u32[]{:S(2)}) copy-start(f32[2,256]{1,0:T(2,128)} %param.6) | copy-start | bytes 6148
Sparse Core Ops, SparseCore 0:
  10.8 2137.7 all-reduce.1
  2177.4 73.6 reduce-scatter.1
where the time goes:
time: 2260 us
  waiting for transfers between devices  2230 us (99%)
    psum x1, waiting for transfers between devices, shards(): summed = lax.psum(adjoint, 'col')  2140 us
    reduce_scatter x1, waiting for transfers between devices, shards(): lax.psum_scatter(jnp.stack(parts, axis=1).astype(jnp.bfloat16), 'row', sc...  72.9 us
  transfers between devices with their start and end apart: 6, of which 6 were waited for; matrix products, arithmetic and copies ran while one was open for 0% of the time, Pallas kernels for 0%

commit v1 on v0

v1 whole, which is shorter than its diff:
```python
import functools

import jax
import jax.numpy as jnp
from jax import lax
from jax.experimental import pallas as pl
from jax.experimental.pallas import tpu as pltpu
from jax.sharding import PartitionSpec as P

F32 = jnp.float32
BF16 = jnp.bfloat16
MESH = pl.DeviceIdType.MESH


def nt(a, b):
    return lax.dot_general(a, b, (((1,), (1,)), ((), ())), preferred_element_type=F32)


def nn(a, b):
    return jnp.dot(a, b, preferred_element_type=F32)


def body(
    n_row, n_col,
    k_hbm, v_hbm, nv_ref, d_ref, o_ref,
    kv, vv, kh, dsend, dh, kp, s0, r0, ao, s1, r1, zs, zr, fc, g, hs, r2, l2s, r3,
    load_sem, halo_s, halo_r, core_s, core_r, rs_s, rs_r, z_s, z_r, ag_s, ag_r, cag_s, cag_r,
    h_s, h_r, l2_sem, l2_r,
):
    row = lax.axis_index("row")
    col = lax.axis_index("col")
    n_xy = n_col // 4
    n_j = n_row // 2
    core = lax.rem(col, 2)
    zh = lax.rem(lax.div(col, 2), 2)
    cxy = lax.div(col, 4)
    half = lax.div(row, n_j)
    j = lax.rem(row, n_j)
    n_cb = 512 // n_xy
    pw = 256 // n_row
    other = 1 - core

    sib = (row, cxy * 4 + zh * 2 + other)
    zpart = (row, cxy * 4 + (1 - zh) * 2 + core)

    def xy_dev(k):
        t = lax.rem(cxy + k, n_xy)
        return t, (row, t * 4 + zh * 2 + core)

    def remote(src, dst, ss, rs, dev):
        return pltpu.make_async_remote_copy(
            src_ref=src, dst_ref=dst, send_sem=ss, recv_sem=rs, device_id=dev, device_id_type=MESH
        )

    barrier = pltpu.get_barrier_semaphore()

    def signal(dev):
        pl.semaphore_signal(barrier, inc=1, device_id=dev, device_id_type=MESH)

    load_k = pltpu.make_async_copy(k_hbm, kv, load_sem.at[0])
    load_v = pltpu.make_async_copy(v_hbm, vv, load_sem.at[1])
    load_k.start()
    load_v.start()
    signal(zpart)
    signal(sib)

    def sig_xy(k, c):
        signal(xy_dev(k)[1])
        return c

    lax.fori_loop(1, n_xy, sig_xy, 0)

    def sig_row(k, c):
        signal((lax.rem(row + k, n_row), col))
        return c

    lax.fori_loop(1, n_row, sig_row, 0)

    dsend[0] = jnp.broadcast_to(d_ref[:, 128:256], (8, 128))
    dsend[1] = jnp.broadcast_to(d_ref[:, 0:128], (8, 128))
    load_k.wait()
    load_v.wait()

    def adjoint(f):
        base = pl.multiple_of(f * 512, 512)
        vr = vv[pl.ds(base, 256), :]
        vi = vv[pl.ds(base + 256, 256), :]
        kr = kv[pl.ds(base, 256), :]
        ki = kv[pl.ds(base + 256, 256), :]
        return nn(vr, kr) + nn(vi, ki), nn(vi, kr) - nn(vr, ki)

    re, im = adjoint(other)
    s0[0:256, :] = re.astype(BF16)
    s0[256:512, :] = im.astype(BF16)
    pl.semaphore_wait(barrier, n_xy - 1 + n_row - 1 + 2)
    core_rs = remote(s0, r0, core_s, core_r, sib)
    core_rs.start()
    re, im = adjoint(core)
    ao[0:256, :] = re
    ao[256:512, :] = im

    up_dev = (jnp.minimum(row + 1, n_row - 1), col)
    down_dev = (jnp.maximum(row - 1, 0), col)
    up = [
        remote(kv.at[:, pl.ds(128, 128)], kh.at[0], halo_s.at[0], halo_r.at[0], up_dev),
        remote(dsend.at[0], dh.at[0], halo_s.at[1], halo_r.at[1], up_dev),
    ]
    down = [
        remote(kv.at[:, pl.ds(0, 128)], kh.at[1], halo_s.at[2], halo_r.at[2], down_dev),
        remote(dsend.at[1], dh.at[1], halo_s.at[3], halo_r.at[3], down_dev),
    ]

    @pl.when(row < n_row - 1)
    def _():
        for cp in up:
            cp.start()

    @pl.when(row > 0)
    def _():
        for cp in down:
            cp.start()

    core_rs.wait_recv()
    s1[...] = (ao[...] + r0[...].astype(F32)).astype(BF16)

    def chunk(t):
        return pl.ds(pl.multiple_of(t * n_cb, n_cb), n_cb)

    def rs_copy(k):
        t, dev = xy_dev(k)
        return remote(s1.at[chunk(t)], r1.at[chunk(cxy)], rs_s, rs_r, dev)

    def rs_start(k, c):
        rs_copy(k).start()
        return c

    lax.fori_loop(1, n_xy, rs_start, 0)
    r1[chunk(cxy), :] = s1[chunk(cxy), :]

    @pl.when(row > 0)
    def _():
        remote(kv.at[:, pl.ds(128, 128)], kh.at[0], halo_s.at[0], halo_r.at[0], up_dev).wait_recv()
        remote(dsend.at[0], dh.at[0], halo_s.at[1], halo_r.at[1], up_dev).wait_recv()

    @pl.when(row < n_row - 1)
    def _():
        remote(kv.at[:, pl.ds(0, 128)], kh.at[1], halo_s.at[2], halo_r.at[2], down_dev).wait_recv()
        remote(dsend.at[1], dh.at[1], halo_s.at[3], halo_r.at[3], down_dev).wait_recv()

    @pl.when(row == 0)
    def _():
        kh[0] = jnp.zeros((1024, 128), BF16)
        dh[0] = jnp.zeros((8, 128), F32)

    @pl.when(row == n_row - 1)
    def _():
        kh[1] = jnp.zeros((1024, 128), BF16)
        dh[1] = jnp.zeros((8, 128), F32)

    coef = jnp.concatenate([dh[0, 0:1, :], d_ref[...], dh[1, 0:1, :]], axis=1)
    lane = lax.broadcasted_iota(jnp.int32, (1, 512), 1)
    low = jnp.where(row > 0, 0, 128)
    high = jnp.where(row < n_row - 1, 512, 384)
    inside = jnp.where((lane >= low) & (lane < high), 1.0, 0.0).astype(F32)

    def stencil(i, c):
        rows = pl.ds(pl.multiple_of(i * 32, 32), 32)
        e = jnp.concatenate([kh[0, rows, :], kv[rows, :], kh[1, rows, :]], axis=1).astype(F32)
        for _ in range(2):
            e = inside * (coef * e - pltpu.roll(e, 1, 1) - pltpu.roll(e, 511, 1))
        kp[rows, :] = e[:, 128:384].astype(BF16)
        return c

    lax.fori_loop(0, 32, stencil, 0)

    span = pl.ds(0, (n_xy - 1) * n_cb)
    remote(r1.at[span], r1.at[span], rs_s, rs_r, sib).wait_recv()
    acc = r1[0:n_cb, :].astype(F32)
    for s in range(1, n_xy):
        acc = acc + r1[s * n_cb:(s + 1) * n_cb, :].astype(F32)

    zs[...] = acc.astype(BF16)
    z_copy = remote(zs, zr, z_s, z_r, zpart)
    z_copy.start()
    z_copy.wait_recv()
    final = (acc + zr[...].astype(F32)).astype(BF16)
    fc[...] = final

    def ag_copy(k):
        _, dev = xy_dev(k)
        return remote(fc, g.at[core, chunk(cxy)], ag_s, ag_r, dev)

    def ag_start(k, c):
        ag_copy(k).start()
        return c

    lax.fori_loop(1, n_xy, ag_start, 0)
    g[core, chunk(cxy), :] = final
    remote(r1.at[span], g.at[core, span], ag_s, ag_r, sib).wait_recv()
    cag = remote(g.at[core], g.at[core], cag_s, cag_r, sib)
    cag.start()

    def row_dev(jt):
        return (half * n_j + jt, col)

    def forward(f):
        base = pl.multiple_of(f * 512, 512)
        kr = kp[pl.ds(base, 256), :]
        ki = kp[pl.ds(base + 256, 256), :]
        for q in (1 - half, half):
            first = pl.multiple_of(q * 128, 128)
            ar = g[f, pl.ds(first, 128), :]
            ai = g[f, pl.ds(first + 256, 128), :]
            hr = (nt(ar, kr) - nt(ai, ki)).astype(BF16)
            hi = (nt(ar, ki) + nt(ai, kr)).astype(BF16)
            for jj in range(n_j):
                hs[q, f, jj, 0:pw, :] = hr[jj * pw:(jj + 1) * pw, :]
                hs[q, f, jj, pw:2 * pw, :] = hi[jj * pw:(jj + 1) * pw, :]

            for k in range(1, n_j):
                jt = lax.rem(j + k, n_j)
                remote(
                    hs.at[q, f, jt], r2.at[q, f, k - 1], h_s.at[q, f], h_r.at[q, f], row_dev(jt)
                ).start()

    def half_sum(q, f):
        remote(r2.at[q, f], r2.at[q, f], h_s.at[q, f], h_r.at[q, f], sib).wait_recv()
        total = hs[q, f, j].astype(F32)
        for k in range(n_j - 1):
            total = total + r2[q, f, k].astype(F32)
        return total

    def across(f):
        return remote(l2s.at[f], r3.at[f], l2_sem.at[f], l2_r.at[f], ((1 - half) * n_j + j, col))

    forward(core)
    remote(g.at[other], g.at[other], cag_s, cag_r, sib).wait_recv()
    forward(other)
    for f in (core, other):
        l2s[f] = half_sum(1 - half, f).astype(BF16)
        across(f).start()
    for f in (core, other):
        total = half_sum(half, f)
        across(f).wait_recv()
        total = total + r3[f].astype(F32)
        level = nv_ref[pl.ds(f, 1), :]
        for c in range(2):
            own = vv[pl.ds(pl.multiple_of(f * 512 + c * 256 + row * pw, pw), pw), :].astype(F32)
            o_ref[pl.ds(pl.multiple_of((f * 2 + c) * pw, pw), pw), :] = (
                total[c * pw:(c + 1) * pw, :] + level * own
            )

    core_rs.wait_send()

    @pl.when(row < n_row - 1)
    def _():
        for cp in up:
            cp.wait_send()

    @pl.when(row > 0)
    def _():
        for cp in down:
            cp.wait_send()

    remote(r1.at[span], r1.at[span], rs_s, rs_r, sib).wait_send()
    z_copy.wait_send()
    remote(r1.at[span], r1.at[span], ag_s, ag_r, sib).wait_send()
    cag.wait_send()
    for f in range(2):
        for q in range(2):
            remote(r2.at[q, f], r2.at[q, f], h_s.at[q, f], h_r.at[q, f], sib).wait_send()
        across(f).wait_send()


def shards(kernel, probes, noise_var, prior_diag):
    n_row = lax.axis_size("row")
    n_col = lax.axis_size("col")
    n_j = n_row // 2
    pw = 256 // n_row
    n_cb = 512 // (n_col // 4)
    v = jnp.transpose(probes, (1, 2, 0, 3)).reshape(1024, 256)
    k = kernel.reshape(1024, 256)
    vmem = pl.BlockSpec(memory_space=pltpu.VMEM)
    hbm = pl.BlockSpec(memory_space=pl.ANY)
    dma = pltpu.SemaphoreType.DMA
    out = pl.pallas_call(
        functools.partial(body, n_row, n_col),
        out_shape=jax.ShapeDtypeStruct((4 * pw, 256), F32),
        in_specs=[hbm, hbm, vmem, vmem],
        out_specs=vmem,
        scratch_shapes=[
            pltpu.VMEM((1024, 256), BF16),
            pltpu.VMEM((1024, 256), BF16),
            pltpu.VMEM((2, 1024, 128), BF16),
            pltpu.VMEM((2, 8, 128), F32),
            pltpu.VMEM((2, 8, 128), F32),
            pltpu.VMEM((1024, 256), BF16),
            pltpu.VMEM((512, 256), BF16),
            pltpu.VMEM((512, 256), BF16),
            pltpu.VMEM((512, 256), F32),
            pltpu.VMEM((512, 256), BF16),
            pltpu.VMEM((512, 256), BF16),
            pltpu.VMEM((n_cb, 256), BF16),
            pltpu.VMEM((n_cb, 256), BF16),
            pltpu.VMEM((n_cb, 256), BF16),
            pltpu.VMEM((2, 512, 256), BF16),
            pltpu.VMEM((2, 2, n_j, 2 * pw, 256), BF16),
            pltpu.VMEM((2, 2, n_j - 1, 2 * pw, 256), BF16),
            pltpu.VMEM((2, 2 * pw, 256), BF16),
            pltpu.VMEM((2, 2 * pw, 256), BF16),
            dma((2,)), dma((4,)), dma((4,)), dma, dma, dma, dma, dma, dma, dma, dma, dma, dma,
            dma((2, 2)), dma((2, 2)), dma((2,)), dma((2,)),
        ],
        compiler_params=pltpu.CompilerParams(
            collective_id=0, has_side_effects=True, vmem_limit_bytes=32 * 1024 * 1024
        ),
    )(k, v, noise_var, prior_diag.reshape(1, 256))
    return jnp.transpose(out.reshape(2, 2, pw, 256), (2, 0, 1, 3))


def solution(mesh):
    in_specs = (P(None, None, "col", "row"), P(None, None, None, "col"), P(None, "col"), P("row"))
    out_specs = P("row", None, None, "col")
    return jax.shard_map(shards, mesh=mesh, in_specs=in_specs, out_specs=out_specs, check_vma=False)
```

time: 2260 us -> 72.4 us (0.03)
  waiting for transfers between devices: 2230 us -> 0 us
  Pallas kernels: 0 us -> 69.6 us
    psum x1 -> x0, waiting for transfers between devices: 2140 us -> none  [shards(): summed = lax.psum(adjoint, 'col')]
    reduce_scatter x1 -> x0, waiting for transfers between devices: 72.9 us -> none  [shards(): lax.psum_scatter(jnp.stack(parts, axis=1).astype(jnp.bfloat16), 'row', sc...]
    pallas_call x0 -> x1, Pallas kernels: none -> 69.6 us  [shards(): pl.pallas_call(functools.partial(body, n_row, n_col), out_shape=jax.Shape...]
  transfers between devices with their start and end apart: 6 -> 0, of which waited for: 6 -> 0; matrix products, arithmetic and copies ran while one was open for 0% -> 0% of each run, Pallas kernels for 0% -> 0%
where the time goes in v1:
time: 72.4 us; the launch traced here: 72.2 us
  Pallas kernels  69.6 us (96%)
  local copies, waits for them, and re-layouts  2.6 us (4%)
    pallas_call x1, Pallas kernels, shards(): pl.pallas_call(functools.partial(body, n_row, n_col), out_shape=jax.Shape...  69.6 us

profile of v1, /device:TPU:2, one launch (start us, length us, event | category | flops | bytes accessed | tf_op | source)
XLA Modules:
  0.0 72.2 jit_solution(9360564092165120539)
XLA Ops:
  0.0 0.0 copy-start
  0.0 0.0 copy-start.1
  0.0 1.2 %copy.5 = bf16[2,2,256,256]{3,2,1,0:T(8,128)(2,1)S(1)} copy(bf16[2,2,256,256]{3,1,0,2:T(2,128)(2,1)} %bitcast.12) | data formatting | bytes 1048576 | tf_op jit(solution)/shard_map/transpose | solution.py:281
  1.2 0.0 copy-start.2
  1.2 0.0 copy-done
  1.2 0.0 copy-done.1
  1.2 0.7 copy-done.2
  1.9 69.6 %shard_map.46 = f32[128,256]{1,0:T(8,128)S(1)} custom-call(bf16[1024,256]{1,0:T(8,128)(2,1)S(1)} %bitcast.9, bf16[1024,256]{1,0:T(8,128)(2,1)S(1)} %bitcast.8, f32[2,256]{1,0:T(2,128)S(1)} %copy-done.1, f32[1,256]{1,0:T(1,128)S(1)} %bitcast.11), custom_call_target="tpu_custom_call" | custom-call | tf_op jit(solution)/shard_map/pallas_call | solution.py:286
  71.4 0.8 %copy.8 = f32[2,2,32,256]{3,1,0,2:T(2,128)} copy(f32[2,2,32,256]{3,2,1,0:T(8,128)S(1)} %bitcast.10) | data formatting | bytes 262144 | tf_op jit(solution)/shard_map/reshape | solution.py:318
Async XLA Ops:
  0.0 1.2 %copy-start = (bf16[2,2,256,256]{3,2,1,0:T(8,128)(2,1)S(1)}, bf16[2,2,256,256]{3,2,1,0:T(8,128)(2,1)}, u32[]{:S(2)}) copy-start(bf16[2,2,256,256]{3,2,1,0:T(8,128)(2,1)} %param.4) | copy-start | bytes 1572868
  0.0 1.2 %copy-start.1 = (f32[2,256]{1,0:T(2,128)S(1)}, f32[2,256]{1,0:T(2,128)}, u32[]{:S(2)}) copy-start(f32[2,256]{1,0:T(2,128)} %nv_ref.1) | copy-start | bytes 6148
  1.2 0.7 copy-start.2

commit v2 on v1

v2 whole, which is shorter than its diff:
```python
import functools

import jax
import jax.numpy as jnp
from jax import lax
from jax.experimental import pallas as pl
from jax.experimental.pallas import tpu as pltpu
from jax.sharding import PartitionSpec as P

F32 = jnp.float32
BF16 = jnp.bfloat16
MESH = pl.DeviceIdType.MESH


def nt(a, b):
    return lax.dot_general(a, b, (((1,), (1,)), ((), ())), preferred_element_type=F32)


def nn(a, b):
    return jnp.dot(a, b, preferred_element_type=F32)


def body(
    n_row, n_col,
    k_hbm, v_hbm, nv_hbm, d_hbm, o_ref,
    kv, vraw, vv, nv_ref, d_ref, kh, dsend, dh, kp, s0, r0, ao, s1, r1, zs, zr, fc, g, hs, r2, rg, l2s, rc,
    load_sem, halo_s, halo_r, core_s, core_r, rs_s, rs_r, z_s, z_r, ag_s, ag_r, cag_s, cag_r,
    kx_s, kx_r, h_s, h_r, g_s, g_r, cr_s, cr_r,
):
    row = lax.axis_index("row")
    col = lax.axis_index("col")
    n_xy = n_col // 4
    n_j = n_row // 2
    core = lax.rem(col, 2)
    zh = lax.rem(lax.div(col, 2), 2)
    cxy = lax.div(col, 4)
    half = lax.div(row, n_j)
    j = lax.rem(row, n_j)
    a = lax.div(j, 2)
    b = lax.rem(j, 2)
    n_cb = 512 // n_xy
    pw = 256 // n_row
    other = 1 - core
    batches = (0, 1)

    sib = (row, cxy * 4 + zh * 2 + other)
    pair_row = row + 1 - 2 * b
    pair = (pair_row, col)
    zcol = cxy * 4 + (1 - zh) * 2 + core
    zpart = (row, zcol)
    zpair = (pair_row, zcol)
    mate = (half * n_j + (1 - a) * 2 + b, col)
    beyond = ((1 - half) * n_j + j, col)

    def xy_dev(i):
        step = lax.div(i + 1, 2)
        k = n_xy // 2 + jnp.where(lax.rem(i, 2) == 1, -step, step)
        t = lax.rem(cxy + k, n_xy)
        return t, (row, t * 4 + zh * 2 + core)

    def remote(src, dst, ss, rs, dev):
        return pltpu.make_async_remote_copy(
            src_ref=src, dst_ref=dst, send_sem=ss, recv_sem=rs, device_id=dev, device_id_type=MESH
        )

    barrier = pltpu.get_barrier_semaphore()

    def signal(dev):
        pl.semaphore_signal(barrier, inc=1, device_id=dev, device_id_type=MESH)

    def sig_xy(i, c):
        signal(xy_dev(i)[1])
        return c

    lax.fori_loop(0, n_xy - 1, sig_xy, 0)
    signal(beyond)
    signal(mate)
    signal(pair)
    signal(sib)
    inland = (row > 0) & (row < n_row - 1)

    @pl.when(inland)
    def _():
        signal((row - 1 + 2 * b, col))

    loads = [
        pltpu.make_async_copy(src, dst, load_sem.at[i])
        for i, (src, dst) in enumerate(
            ((v_hbm, vraw), (k_hbm, kv), (d_hbm, d_ref), (nv_hbm, nv_ref))
        )
    ]
    for cp in loads:
        cp.start()

    loads[0].wait()

    def order(i, c):
        for f in range(2):
            x = jnp.swapaxes(vraw[pl.ds(i * 2 * pw, 2 * pw), f].astype(F32), 0, 1)
            x = jnp.swapaxes(x.reshape(2, 2, pw // 8, 8, 256), 1, 2).reshape(2, 2 * pw, 256)
            for part in range(2):
                first = pl.multiple_of((f * 2 + part) * 256 + i * 2 * pw, 2 * pw)
                vv[pl.ds(first, 2 * pw), :] = x[part].astype(BF16)
        return c

    lax.fori_loop(0, n_j, order, 0)
    loads[1].wait()

    def adjoint(f):
        base = pl.multiple_of(f * 512, 512)
        vr = vv[pl.ds(base, 256), :]
        vi = vv[pl.ds(base + 256, 256), :]
        kr = kv[pl.ds(base, 256), :]
        ki = kv[pl.ds(base + 256, 256), :]
        return nn(vr, kr) + nn(vi, ki), nn(vi, kr) - nn(vr, ki)

    def put(ref, parts):
        for c in range(2):
            for q in range(2):
                for h in range(2):
                    ref[q, h, c * 128:(c + 1) * 128, :] = parts[c][
                        q * 128:(q + 1) * 128, h * 128:(h + 1) * 128
                    ].astype(ref.dtype)

    put(s0, adjoint(other))
    met = n_xy - 1 + 4 + jnp.where(inland, 1, 0)
    pl.semaphore_wait(barrier, met + 2 * zh)
    signal(zpart)
    signal(zpair)

    def core_rs(q):
        return remote(s0.at[q], r0.at[q], core_s.at[q], core_r.at[q], sib)

    for q in batches:
        core_rs(q).start()
    loads[2].wait()
    loads[3].wait()
    dsend[0] = jnp.broadcast_to(d_ref[:, 128:256], (8, 128))
    dsend[1] = jnp.broadcast_to(d_ref[:, 0:128], (8, 128))
    up_dev = (jnp.minimum(row + 1, n_row - 1), col)
    down_dev = (jnp.maximum(row - 1, 0), col)
    up = [
        remote(kv.at[:, pl.ds(128, 128)], kh.at[:, pl.ds(0, 128)], halo_s.at[0], halo_r.at[0], up_dev),
        remote(dsend.at[0], dh.at[0], halo_s.at[1], halo_r.at[1], up_dev),
    ]
    down = [
        remote(kv.at[:, pl.ds(0, 128)], kh.at[:, pl.ds(128, 128)], halo_s.at[2], halo_r.at[2], down_dev),
        remote(dsend.at[1], dh.at[1], halo_s.at[3], halo_r.at[3], down_dev),
    ]

    @pl.when(row < n_row - 1)
    def _():
        for cp in up:
            cp.start()

    @pl.when(row > 0)
    def _():
        for cp in down:
            cp.start()

    put(ao, adjoint(core))

    def rows_of(t):
        return pl.ds(pl.multiple_of(lax.div(t, 2) * n_cb, n_cb), n_cb)

    slot = pl.ds(pl.multiple_of(cxy * n_cb, n_cb), n_cb)
    span = pl.ds(0, (n_xy - 1) * n_cb)
    lanes = lax.rem(cxy, 2)

    for q in batches:
        core_rs(q).wait_recv()
        s1[q] = (ao[q] + r0[q].astype(F32)).astype(BF16)

        def rs_start(i, c):
            t, dev = xy_dev(i)
            remote(
                s1.at[q, lax.rem(t, 2), rows_of(t)], r1.at[q, slot], rs_s.at[q], rs_r.at[q], dev
            ).start()
            return c

        lax.fori_loop(0, n_xy - 1, rs_start, 0)
        r1[q, slot, :] = s1[q, lanes, rows_of(cxy), :]

    @pl.when(row > 0)
    def _():
        for cp in up:
            cp.wait_recv()

    @pl.when(row < n_row - 1)
    def _():
        for cp in down:
            cp.wait_recv()

    @pl.when(row == 0)
    def _():
        kh[:, 0:128] = jnp.zeros((1024, 128), BF16)
        dh[0] = jnp.zeros((8, 128), F32)

    @pl.when(row == n_row - 1)
    def _():
        kh[:, 128:256] = jnp.zeros((1024, 128), BF16)
        dh[1] = jnp.zeros((8, 128), F32)

    lane = lax.broadcasted_iota(jnp.int32, (256, 256), 1)
    depth = lax.broadcasted_iota(jnp.int32, (256, 256), 0)
    d = d_ref[...]
    before = jnp.concatenate([dh[0, 0:1, :], d, dh[1, 0:1, :]], axis=1)
    left = pltpu.roll(before, 1, 1)[:, 128:384]
    right = pltpu.roll(before, 511, 1)[:, 128:384]
    ends = (lane == 0) & (row == 0) | (lane == 255) & (row == n_row - 1)

    def banded(gap):
        m = jnp.where(gap == 0, d * d + jnp.where(ends, 1.0, 2.0), 0.0)
        m = jnp.where(gap == -1, -(left + d), m)
        m = jnp.where(gap == 1, -(right + d), m)
        return jnp.where((gap == 2) | (gap == -2), 1.0, m)

    def thirds(m):
        a = m.astype(BF16)
        rest = m - a.astype(F32)
        b = rest.astype(BF16)
        return a, b, (rest - b.astype(F32)).astype(BF16)

    inner = thirds(banded(depth - lane))
    outer = thirds(banded(jnp.where(depth < 128, depth - 128, depth + 128) - lane))
    for i in range(0, 1024, 256):
        e = kv[i:i + 256, :]
        h = kh[i:i + 256, :]
        total = nn(e, inner[0]) + nn(h, outer[0])
        total = total + (nn(e, inner[1]) + nn(h, outer[1]))
        total = total + (nn(e, inner[2]) + nn(h, outer[2]))
        kp[b, i:i + 256, :] = total.astype(BF16)

    def swap(f):
        part = kp.at[b, pl.ds(pl.multiple_of(f * 512, 512), 512)]
        return remote(part, part, kx_s.at[f], kx_r.at[f], pair)


    def z_copies(q):
        return [
            remote(zs.at[q], zr.at[q, i], z_s.at[q], z_r.at[q], dev)
            for i, dev in enumerate((zpart, zpair, pair))
        ]

    def z_all(q):
        return remote(zr.at[q], zr.at[q], z_s.at[q], z_r.at[q], sib)

    @pl.when(zh == 0)
    def _():
        pl.semaphore_wait(barrier, 2)

    own = []
    for q in batches:
        remote(r1.at[q, span], r1.at[q, span], rs_s.at[q], rs_r.at[q], sib).wait_recv()
        acc = r1[q, 0:n_cb, :].astype(F32)
        for s in range(1, n_xy):
            acc = acc + r1[q, s * n_cb:(s + 1) * n_cb, :].astype(F32)
        zs[q] = acc.astype(BF16)
        for cp in z_copies(q):
            cp.start()
        own.append(acc)

    swap(core).start()

    @pl.when(zh == 0)
    def _():
        swap(other).start()

    for q, acc in zip(batches, own):
        z_all(q).wait_recv()

        def share(x):
            return jnp.where(b == 0, x[0:8, :], x[8:16, :])

        mine = share(acc + zr[q, 0].astype(F32))
        theirs = share(zr[q, 1].astype(F32) + zr[q, 2].astype(F32))
        even = jnp.where(b == 0, mine, theirs)
        odd = jnp.where(b == 0, theirs, mine)
        final = jnp.concatenate([even, odd], axis=0).astype(BF16)
        fc[q] = final

        def ag_start(i, c):
            _, dev = xy_dev(i)
            remote(
                fc.at[q], g.at[core, q, lanes, rows_of(cxy)], ag_s.at[q], ag_r.at[q], dev
            ).start()
            return c

        lax.fori_loop(0, n_xy - 1, ag_start, 0)
        g[core, q, lanes, rows_of(cxy), :] = final

    @pl.when(zh == 1)
    def _():
        swap(other).start()

    def cag(f, q):
        return remote(g.at[f, q], g.at[f, q], cag_s.at[q], cag_r.at[q], sib)

    def forward(f, q):
        base = pl.multiple_of(f * 512, 512)
        both = jnp.concatenate([g[f, q, 0], g[f, q, 1]], axis=1).astype(F32).reshape(16, 2, 8, 256)
        real = imag = 0.0
        for block in range(2):
            x = both[:, block].reshape(128, 256).astype(BF16)
            real = real + nt(x, kp[block, pl.ds(base, 256), :])
            imag = imag + nt(x, kp[block, pl.ds(base + 256, 256), :])
        hr = (real[0:64, :] - imag[64:128, :]).astype(BF16)
        hi = (imag[0:64, :] + real[64:128, :]).astype(BF16)
        for aa in range(2):
            hs[q, f, aa, 0:pw, :] = hr[aa * pw:(aa + 1) * pw, :]
            hs[q, f, aa, pw:2 * pw, :] = hi[aa * pw:(aa + 1) * pw, :]

        @pl.when(q == half)
        def _():
            near(f).start()

        @pl.when((q != half) & (a == 1))
        def _():
            give(f).start()

    def near(f):
        return remote(hs.at[half, f, 1 - a], r2.at[f], h_s.at[f], h_r.at[f], mate)

    def give(f):
        return remote(hs.at[1 - half, f, 1 - a], rg.at[f], g_s.at[f], g_r.at[f], mate)

    def across(f):
        return remote(l2s.at[f], rc.at[f], cr_s.at[f], cr_r.at[f], beyond)

    def cross(giving):
        for f in (core, other):
            give(f).wait_recv()
            l2s[f] = (hs[1 - half, f, a].astype(F32) + rg[f].astype(F32)).astype(BF16)
            across(f).start()
            if giving:
                give(f).start()

    for q in batches:
        remote(r1.at[q, span], r1.at[q, span], ag_s.at[q], ag_r.at[q], sib).wait_recv()
        cag(core, q).start()
        if q == 0:
            swap(core).wait_recv()
        forward(core, q)
        cag(other, q).wait_recv()
        if q == 0:
            swap(other).wait_recv()
        forward(other, q)

        @pl.when((q != half) & (a == 0))
        def _():
            cross(True)

    @pl.when(a == 1)
    def _():
        cross(False)

    for f in (core, other):
        near(f).wait_recv()
        total = hs[half, f, a].astype(F32) + r2[f].astype(F32)
        across(f).wait_recv()
        total = total + rc[f].astype(F32)
        level = nv_ref[pl.ds(f, 1), :]
        for c in range(2):
            first = pl.multiple_of(f * 512 + c * 256 + half * 128 + a * 64, 64)
            block = vv[pl.ds(first, 2 * pw), :].astype(F32).reshape(pw // 8, 2, 8, 256)
            mine = jnp.where(b == 0, block[:, 0], block[:, 1]).reshape(pw, 256)
            o_ref[pl.ds(pl.multiple_of((f * 2 + c) * pw, pw), pw), :] = (
                total[c * pw:(c + 1) * pw, :] + level * mine
            )

    @pl.when(row < n_row - 1)
    def _():
        for cp in up:
            cp.wait_send()

    @pl.when(row > 0)
    def _():
        for cp in down:
            cp.wait_send()

    for q in range(2):
        core_rs(q).wait_send()
        remote(r1.at[q, span], r1.at[q, span], rs_s.at[q], rs_r.at[q], sib).wait_send()
        z_all(q).wait_send()
        remote(r1.at[q, span], r1.at[q, span], ag_s.at[q], ag_r.at[q], sib).wait_send()
        cag(core, q).wait_send()
        swap(q).wait_send()
        near(q).wait_send()
        give(q).wait_send()
        across(q).wait_send()


def shards(kernel, probes, noise_var, prior_diag):
    n_row = lax.axis_size("row")
    n_col = lax.axis_size("col")
    n_j = n_row // 2
    pw = 256 // n_row
    n_cb = 512 // (n_col // 4)
    k = kernel.reshape(1024, 256)
    vmem = pl.BlockSpec(memory_space=pltpu.VMEM)
    hbm = pl.BlockSpec(memory_space=pltpu.HBM)
    dma = pltpu.SemaphoreType.DMA
    out = pl.pallas_call(
        functools.partial(body, n_row, n_col),
        out_shape=jax.ShapeDtypeStruct((4 * pw, 256), F32),
        in_specs=[hbm, hbm, hbm, hbm],
        out_specs=vmem,
        scratch_shapes=[
            pltpu.VMEM((1024, 256), BF16),
            pltpu.VMEM((256, 2, 2, 256), BF16),
            pltpu.VMEM((1024, 256), BF16),
            pltpu.VMEM((2, 256), F32),
            pltpu.VMEM((1, 256), F32),
            pltpu.VMEM((1024, 256), BF16),
            pltpu.VMEM((2, 8, 128), F32),
            pltpu.VMEM((2, 8, 128), F32),
            pltpu.VMEM((2, 1024, 256), BF16),
            pltpu.VMEM((2, 2, 256, 128), BF16),
            pltpu.VMEM((2, 2, 256, 128), BF16),
            pltpu.VMEM((2, 2, 256, 128), F32),
            pltpu.VMEM((2, 2, 256, 128), BF16),
            pltpu.VMEM((2, 512, 128), BF16),
            pltpu.VMEM((2, n_cb, 128), BF16),
            pltpu.VMEM((2, 3, n_cb, 128), BF16),
            pltpu.VMEM((2, n_cb, 128), BF16),
            pltpu.VMEM((2, 2, 2, 256, 128), BF16),
            pltpu.VMEM((2, 2, n_j // 2, 2 * pw, 256), BF16),
            pltpu.VMEM((2, 2 * pw, 256), BF16),
            pltpu.VMEM((2, 2 * pw, 256), BF16),
            pltpu.VMEM((2, 2 * pw, 256), BF16),
            pltpu.VMEM((2, 2 * pw, 256), BF16),
            dma((4,)), dma((4,)), dma((4,)), dma((2,)), dma((2,)), dma((2,)), dma((2,)), dma((2,)),
            dma((2,)), dma((2,)), dma((2,)), dma((2,)), dma((2,)),
            dma((2,)), dma((2,)), dma((2,)), dma((2,)), dma((2,)), dma((2,)), dma((2,)), dma((2,)),
        ],
        compiler_params=pltpu.CompilerParams(
            collective_id=0, has_side_effects=True, vmem_limit_bytes=60 * 1024 * 1024
        ),
    )(k, probes, noise_var, prior_diag.reshape(1, 256))
    return jnp.transpose(out.reshape(2, 2, pw, 256), (2, 0, 1, 3))


def solution(mesh):
    in_specs = (P(None, None, "col", "row"), P(None, None, None, "col"), P(None, "col"), P("row"))
    out_specs = P("row", None, None, "col")
    return jax.shard_map(shards, mesh=mesh, in_specs=in_specs, out_specs=out_specs, check_vma=False)
```

time: 72.4 us -> 61.7 us (0.85)
  the two profiles are of different devices: /device:TPU:2 before, /device:TPU:134 now
where the time goes in v2:
time: 61.7 us; the launch traced here: 61.5 us
  Pallas kernels  59.8 us (97%)
  local copies, waits for them, and re-layouts  1.66 us (3%)
    pallas_call x1, Pallas kernels, shards(): pl.pallas_call(functools.partial(body, n_row, n_col), out_shape=jax.Shape...  59.8 us
    reshape x1, local copies, waits for them, and re-layouts, shards(): return jnp.transpose(out.reshape(2, 2, pw, 256), (2, 0, 1, 3))  1.66 us

profile of v2, /device:TPU:134, one launch (start us, length us, event | category | flops | bytes accessed | tf_op | source)
XLA Modules:
  0.0 61.5 jit_solution(612776747363654615)
XLA Ops:
  0.0 59.8 %shard_map.46 = f32[128,256]{1,0:T(8,128)} custom-call(bf16[1024,256]{1,0:T(8,128)(2,1)} %bitcast.6, bf16[256,2,2,256]{3,2,1,0:T(2,128)(2,1)} %v_hbm.1, f32[2,256]{1,0:T(2,128)} %nv_hbm.1, f32[1,256]{1,0:T(1,128)} %bitcast.8), custom_call_target="tpu_custom_call" | custom-call | tf_op jit(solution)/shard_map/pallas_call | solution.py:403
  59.8 1.7 %copy.7 = f32[2,2,32,256]{3,1,0,2:T(2,128)} copy(f32[2,2,32,256]{3,2,1,0:T(8,128)} %bitcast.7) | data formatting | bytes 262144 | tf_op jit(solution)/shard_map/reshape | solution.py:440

commit v3 on v2

--- a/solution.py
+++ b/solution.py
@@ -23,9 +23,9 @@
 def body(
     n_row, n_col,
     k_hbm, v_hbm, nv_hbm, d_hbm, o_ref,
-    kv, vraw, vv, nv_ref, d_ref, kh, dsend, dh, kp, s0, r0, ao, s1, r1, zs, zr, fc, g, hs, r2, rg, l2s, rc,
-    load_sem, halo_s, halo_r, core_s, core_r, rs_s, rs_r, z_s, z_r, ag_s, ag_r, cag_s, cag_r,
-    kx_s, kx_r, h_s, h_r, g_s, g_r, cr_s, cr_r,
+    kv, vraw, vv, nv_ref, d_ref, kh, dsend, dh, ks, kp, s0, r0, ao, s1, r1, zs, zr, fc, g, hs, r2, rg, l2s, rc, rd, xs, rl,
+    load_sem, halo_s, halo_r, core_s, core_r, rs_s, rs_r, z_s, z_r, ag_s, ag_r, kc_s, kc_r,
+    kx_s, kx_r, h_s, h_r, g_s, g_r, cr_s, cr_r, fa_s, fa_r, lo_s, lo_r,
 ):
     row = lax.axis_index("row")
     col = lax.axis_index("col")
@@ -42,6 +42,7 @@
     pw = 256 // n_row
     other = 1 - core
     batches = (0, 1)
+    order_of_rows = (1, 0)
 
     sib = (row, cxy * 4 + zh * 2 + other)
     pair_row = row + 1 - 2 * b
@@ -51,6 +52,10 @@
     zpair = (pair_row, zcol)
     mate = (half * n_j + (1 - a) * 2 + b, col)
     beyond = ((1 - half) * n_j + j, col)
+    aslant = ((1 - half) * n_j + (1 - a) * 2 + b, col)
+
+    def col_of(r):
+        return cxy * 4 + zh * 2 + r
 
     def xy_dev(i):
         step = lax.div(i + 1, 2)
@@ -74,7 +79,11 @@
 
     lax.fori_loop(0, n_xy - 1, sig_xy, 0)
     signal(beyond)
+    signal(aslant)
+    signal((aslant[0], col_of(other)))
     signal(mate)
+    signal((beyond[0], col_of(other)))
+    signal((mate[0], col_of(other)))
     signal(pair)
     signal(sib)
     inland = (row > 0) & (row < n_row - 1)
@@ -123,7 +132,7 @@
                     ].astype(ref.dtype)
 
     put(s0, adjoint(other))
-    met = n_xy - 1 + 4 + jnp.where(inland, 1, 0)
+    met = n_xy - 1 + 8 + jnp.where(inland, 1, 0)
     pl.semaphore_wait(barrier, met + 2 * zh)
     signal(zpart)
     signal(zpair)
@@ -223,18 +232,25 @@
 
     inner = thirds(banded(depth - lane))
     outer = thirds(banded(jnp.where(depth < 128, depth - 128, depth + 128) - lane))
-    for i in range(0, 1024, 256):
-        e = kv[i:i + 256, :]
-        h = kh[i:i + 256, :]
+
+    def smooth(f, part):
+        rows = pl.ds(pl.multiple_of(f * 512 + part * 256, 256), 256)
+        e = kv[rows, :]
+        h = kh[rows, :]
         total = nn(e, inner[0]) + nn(h, outer[0])
         total = total + (nn(e, inner[1]) + nn(h, outer[1]))
         total = total + (nn(e, inner[2]) + nn(h, outer[2]))
-        kp[b, i:i + 256, :] = total.astype(BF16)
-
-    def swap(f):
-        part = kp.at[b, pl.ds(pl.multiple_of(f * 512, 512), 512)]
-        return remote(part, part, kx_s.at[f], kx_r.at[f], pair)
-
+        return total.astype(BF16)
+
+    core_swap = remote(ks, kp.at[b, core], kc_s, kc_r, sib)
+    for part in range(2):
+        ks[part * 256:(part + 1) * 256, :] = smooth(other, part)
+    core_swap.start()
+    for part in range(2):
+        kp[b, core, part * 256:(part + 1) * 256, :] = smooth(core, part)
+
+    def swap(r):
+        return remote(kp.at[b, r], kp.at[b, r], kx_s.at[r], kx_r.at[r], pair)
 
     def z_copies(q):
         return [
@@ -261,6 +277,7 @@
         own.append(acc)
 
     swap(core).start()
+    core_swap.wait_recv()
 
     @pl.when(zh == 0)
     def _():
@@ -282,83 +299,104 @@
         def ag_start(i, c):
             _, dev = xy_dev(i)
             remote(
-                fc.at[q], g.at[core, q, lanes, rows_of(cxy)], ag_s.at[q], ag_r.at[q], dev
+                fc.at[q], g.at[q, lanes, rows_of(cxy)], ag_s.at[q], ag_r.at[q], dev
             ).start()
             return c
 
         lax.fori_loop(0, n_xy - 1, ag_start, 0)
-        g[core, q, lanes, rows_of(cxy), :] = final
+        g[q, lanes, rows_of(cxy), :] = final
 
     @pl.when(zh == 1)
     def _():
         swap(other).start()
 
-    def cag(f, q):
-        return remote(g.at[f, q], g.at[f, q], cag_s.at[q], cag_r.at[q], sib)
-
-    def forward(f, q):
-        base = pl.multiple_of(f * 512, 512)
-        both = jnp.concatenate([g[f, q, 0], g[f, q, 1]], axis=1).astype(F32).reshape(16, 2, 8, 256)
+    def forward(r, q):
+        both = jnp.concatenate([g[q, 0], g[q, 1]], axis=1).astype(F32).reshape(16, 2, 8, 256)
         real = imag = 0.0
         for block in range(2):
             x = both[:, block].reshape(128, 256).astype(BF16)
-            real = real + nt(x, kp[block, pl.ds(base, 256), :])
-            imag = imag + nt(x, kp[block, pl.ds(base + 256, 256), :])
+            real = real + nt(x, kp[block, r, 0:256, :])
+            imag = imag + nt(x, kp[block, r, 256:512, :])
         hr = (real[0:64, :] - imag[64:128, :]).astype(BF16)
         hi = (imag[0:64, :] + real[64:128, :]).astype(BF16)
         for aa in range(2):
-            hs[q, f, aa, 0:pw, :] = hr[aa * pw:(aa + 1) * pw, :]
-            hs[q, f, aa, pw:2 * pw, :] = hi[aa * pw:(aa + 1) * pw, :]
+            hs[q, r, aa, 0:pw, :] = hr[aa * pw:(aa + 1) * pw, :]
+            hs[q, r, aa, pw:2 * pw, :] = hi[aa * pw:(aa + 1) * pw, :]
 
         @pl.when(q == half)
         def _():
-            near(f).start()
+            near(r).start()
 
         @pl.when((q != half) & (a == 1))
         def _():
-            give(f).start()
-
-    def near(f):
-        return remote(hs.at[half, f, 1 - a], r2.at[f], h_s.at[f], h_r.at[f], mate)
-
-    def give(f):
-        return remote(hs.at[1 - half, f, 1 - a], rg.at[f], g_s.at[f], g_r.at[f], mate)
-
-    def across(f):
-        return remote(l2s.at[f], rc.at[f], cr_s.at[f], cr_r.at[f], beyond)
-
-    def cross(giving):
-        for f in (core, other):
-            give(f).wait_recv()
-            l2s[f] = (hs[1 - half, f, a].astype(F32) + rg[f].astype(F32)).astype(BF16)
-            across(f).start()
-            if giving:
-                give(f).start()
+            give(r).start()
+
+        @pl.when(q != half)
+        def _():
+            far(r).start()
+
+    def near(r):
+        return remote(
+            hs.at[half, r, 1 - a], r2.at[core], h_s.at[r], h_r.at[core], (mate[0], col_of(r))
+        )
+
+    def far(r):
+        return remote(
+            hs.at[1 - half, r, 1], rd.at[core, a], fa_s.at[r], fa_r.at[core],
+            ((1 - half) * n_j + 2 + b, col_of(r)),
+        )
+
+    def give(r):
+        return remote(hs.at[1 - half, r, 0], rg.at[r], g_s.at[r], g_r.at[r], mate)
+
+    def across(r):
+        return remote(l2s.at[r], rc.at[core], cr_s.at[r], cr_r.at[core], (beyond[0], col_of(r)))
+
+    def local():
+        return remote(hs.at[half, other, a], rl, lo_s, lo_r, sib)
+
+    def cross():
+        for r in order_of_rows:
+            give(r).wait_recv()
+            l2s[r] = (hs[1 - half, r, 0].astype(F32) + rg[r].astype(F32)).astype(BF16)
+            across(r).start()
 
     for q in batches:
         remote(r1.at[q, span], r1.at[q, span], ag_s.at[q], ag_r.at[q], sib).wait_recv()
-        cag(core, q).start()
         if q == 0:
             swap(core).wait_recv()
-        forward(core, q)
-        cag(other, q).wait_recv()
-        if q == 0:
             swap(other).wait_recv()
-        forward(other, q)
+        for r in order_of_rows:
+            forward(r, q)
+
+        @pl.when(q == half)
+        def _():
+            local().start()
 
         @pl.when((q != half) & (a == 0))
         def _():
-            cross(True)
-
-    @pl.when(a == 1)
-    def _():
-        cross(False)
+            cross()
 
     for f in (core, other):
-        near(f).wait_recv()
-        total = hs[half, f, a].astype(F32) + r2[f].astype(F32)
-        across(f).wait_recv()
-        total = total + rc[f].astype(F32)
+        if f is core:
+            total = hs[half, core, a].astype(F32)
+        else:
+            local().wait_recv()
+            total = rl[...].astype(F32)
+        remote(r2.at[f], r2.at[f], h_s.at[f], h_r.at[f], sib).wait_recv()
+        total = total + r2[f].astype(F32)
+
+        @pl.when(a == 0)
+        def _():
+            remote(rc.at[f], rc.at[f], cr_s.at[f], cr_r.at[f], sib).wait_recv()
+            xs[...] = rc[f].astype(F32)
+
+        @pl.when(a == 1)
+        def _():
+            remote(rd.at[f], rd.at[f], fa_s.at[f], fa_r.at[f], sib).wait_recv()
+            xs[...] = rd[f, 0].astype(F32) + rd[f, 1].astype(F32)
+
+        total = total + xs[...]
         level = nv_ref[pl.ds(f, 1), :]
         for c in range(2):
             first = pl.multiple_of(f * 512 + c * 256 + half * 128 + a * 64, 64)
@@ -383,11 +421,20 @@
         remote(r1.at[q, span], r1.at[q, span], rs_s.at[q], rs_r.at[q], sib).wait_send()
         z_all(q).wait_send()
         remote(r1.at[q, span], r1.at[q, span], ag_s.at[q], ag_r.at[q], sib).wait_send()
-        cag(core, q).wait_send()
         swap(q).wait_send()
         near(q).wait_send()
-        give(q).wait_send()
-        across(q).wait_send()
+        far(q).wait_send()
+
+        @pl.when(a == 1)
+        def _():
+            give(q).wait_send()
+
+        @pl.when(a == 0)
+        def _():
+            across(q).wait_send()
+
+    core_swap.wait_send()
+    local().wait_send()
 
 
 def shards(kernel, probes, noise_var, prior_diag):
@@ -414,7 +461,8 @@
             pltpu.VMEM((1024, 256), BF16),
             pltpu.VMEM((2, 8, 128), F32),
             pltpu.VMEM((2, 8, 128), F32),
-            pltpu.VMEM((2, 1024, 256), BF16),
+            pltpu.VMEM((512, 256), BF16),
+            pltpu.VMEM((2, 2, 512, 256), BF16),
             pltpu.VMEM((2, 2, 256, 128), BF16),
             pltpu.VMEM((2, 2, 256, 128), BF16),
             pltpu.VMEM((2, 2, 256, 128), F32),
@@ -423,15 +471,19 @@
             pltpu.VMEM((2, n_cb, 128), BF16),
             pltpu.VMEM((2, 3, n_cb, 128), BF16),
             pltpu.VMEM((2, n_cb, 128), BF16),
-            pltpu.VMEM((2, 2, 2, 256, 128), BF16),
+            pltpu.VMEM((2, 2, 256, 128), BF16),
             pltpu.VMEM((2, 2, n_j // 2, 2 * pw, 256), BF16),
             pltpu.VMEM((2, 2 * pw, 256), BF16),
             pltpu.VMEM((2, 2 * pw, 256), BF16),
             pltpu.VMEM((2, 2 * pw, 256), BF16),
             pltpu.VMEM((2, 2 * pw, 256), BF16),
+            pltpu.VMEM((2, 2, 2 * pw, 256), BF16),
+            pltpu.VMEM((2 * pw, 256), F32),
+            pltpu.VMEM((2 * pw, 256), BF16),
             dma((4,)), dma((4,)), dma((4,)), dma((2,)), dma((2,)), dma((2,)), dma((2,)), dma((2,)),
-            dma((2,)), dma((2,)), dma((2,)), dma((2,)), dma((2,)),
+            dma((2,)), dma((2,)), dma((2,)), dma, dma,
             dma((2,)), dma((2,)), dma((2,)), dma((2,)), dma((2,)), dma((2,)), dma((2,)), dma((2,)),
+            dma((2,)), dma((2,)), dma, dma,
         ],
         compiler_params=pltpu.CompilerParams(
             collective_id=0, has_side_effects=True, vmem_limit_bytes=60 * 1024 * 1024

time: 61.7 us -> 61.6 us (level)
  the two profiles are of different devices: /device:TPU:134 before, /device:TPU:8 now
where the time goes in v3:
time: 61.6 us; the launch traced here: 61.4 us
  Pallas kernels  59.7 us (97%)
  local copies, waits for them, and re-layouts  1.66 us (3%)
    pallas_call x1, Pallas kernels, shards(): pl.pallas_call(functools.partial(body, n_row, n_col), out_shape=jax.Shape...  59.7 us
    reshape x1, local copies, waits for them, and re-layouts, shards(): return jnp.transpose(out.reshape(2, 2, pw, 256), (2, 0, 1, 3))  1.66 us

profile of v3, /device:TPU:8, one launch (start us, length us, event | category | flops | bytes accessed | tf_op | source)
XLA Modules:
  0.0 61.4 jit_solution(7132222669364093642)
XLA Ops:
  0.0 59.7 %shard_map.46 = f32[128,256]{1,0:T(8,128)} custom-call(bf16[1024,256]{1,0:T(8,128)(2,1)} %bitcast.6, bf16[256,2,2,256]{3,2,1,0:T(2,128)(2,1)} %v_hbm.1, f32[2,256]{1,0:T(2,128)} %nv_hbm.1, f32[1,256]{1,0:T(1,128)} %bitcast.8), custom_call_target="tpu_custom_call" | custom-call | tf_op jit(solution)/shard_map/pallas_call | solution.py:450
  59.7 1.7 %copy.7 = f32[2,2,32,256]{3,1,0,2:T(2,128)} copy(f32[2,2,32,256]{3,2,1,0:T(8,128)} %bitcast.7) | data formatting | bytes 262144 | tf_op jit(solution)/shard_map/reshape | solution.py:492

commit v4 on v3

--- a/solution.py
+++ b/solution.py
@@ -331,10 +331,6 @@
         def _():
             give(r).start()
 
-        @pl.when(q != half)
-        def _():
-            far(r).start()
-
     def near(r):
         return remote(
             hs.at[half, r, 1 - a], r2.at[core], h_s.at[r], h_r.at[core], (mate[0], col_of(r))
@@ -368,6 +364,11 @@
             swap(other).wait_recv()
         for r in order_of_rows:
             forward(r, q)
+
+        @pl.when(q != half)
+        def _():
+            for r in order_of_rows:
+                far(r).start()
 
         @pl.when(q == half)
         def _():

time: 61.6 us -> 61.4 us (level)
  the two profiles are of different devices: /device:TPU:8 before, /device:TPU:1 now
where the time goes in v4:
time: 61.4 us; the launch traced here: 61.2 us
  Pallas kernels  59.5 us (97%)
  local copies, waits for them, and re-layouts  1.66 us (3%)
    pallas_call x1, Pallas kernels, shards(): pl.pallas_call(functools.partial(body, n_row, n_col), out_shape=jax.Shape...  59.5 us
    reshape x1, local copies, waits for them, and re-layouts, shards(): return jnp.transpose(out.reshape(2, 2, pw, 256), (2, 0, 1, 3))  1.66 us

profile of v4, /device:TPU:1, one launch (start us, length us, event | category | flops | bytes accessed | tf_op | source)
XLA Modules:
  0.0 61.2 jit_solution(6046735934432133047)
XLA Ops:
  0.0 59.5 %shard_map.46 = f32[128,256]{1,0:T(8,128)} custom-call(bf16[1024,256]{1,0:T(8,128)(2,1)} %bitcast.6, bf16[256,2,2,256]{3,2,1,0:T(2,128)(2,1)} %v_hbm.1, f32[2,256]{1,0:T(2,128)} %nv_hbm.1, f32[1,256]{1,0:T(1,128)} %bitcast.8), custom_call_target="tpu_custom_call" | custom-call | tf_op jit(solution)/shard_map/pallas_call | solution.py:451
  59.5 1.7 %copy.7 = f32[2,2,32,256]{3,1,0,2:T(2,128)} copy(f32[2,2,32,256]{3,2,1,0:T(8,128)} %bitcast.7) | data formatting | bytes 262144 | tf_op jit(solution)/shard_map/reshape | solution.py:493

commit v5 on v3

--- a/solution.py
+++ b/solution.py
@@ -23,9 +23,9 @@
 def body(
     n_row, n_col,
     k_hbm, v_hbm, nv_hbm, d_hbm, o_ref,
-    kv, vraw, vv, nv_ref, d_ref, kh, dsend, dh, ks, kp, s0, r0, ao, s1, r1, zs, zr, fc, g, hs, r2, rg, l2s, rc, rd, xs, rl,
+    kv, vraw, vv, nv_ref, d_ref, kh, dsend, dh, ks, kp, s0, r0, ao, s1, r1, zs, zr, fc, g, hs, r2, rg, l2s, rc, rl,
     load_sem, halo_s, halo_r, core_s, core_r, rs_s, rs_r, z_s, z_r, ag_s, ag_r, kc_s, kc_r,
-    kx_s, kx_r, h_s, h_r, g_s, g_r, cr_s, cr_r, fa_s, fa_r, lo_s, lo_r,
+    kx_s, kx_r, h_s, h_r, g_s, g_r, cr_s, cr_r, lo_s, lo_r,
 ):
     row = lax.axis_index("row")
     col = lax.axis_index("col")
@@ -42,7 +42,6 @@
     pw = 256 // n_row
     other = 1 - core
     batches = (0, 1)
-    order_of_rows = (1, 0)
 
     sib = (row, cxy * 4 + zh * 2 + other)
     pair_row = row + 1 - 2 * b
@@ -52,7 +51,6 @@
     zpair = (pair_row, zcol)
     mate = (half * n_j + (1 - a) * 2 + b, col)
     beyond = ((1 - half) * n_j + j, col)
-    aslant = ((1 - half) * n_j + (1 - a) * 2 + b, col)
 
     def col_of(r):
         return cxy * 4 + zh * 2 + r
@@ -79,8 +77,6 @@
 
     lax.fori_loop(0, n_xy - 1, sig_xy, 0)
     signal(beyond)
-    signal(aslant)
-    signal((aslant[0], col_of(other)))
     signal(mate)
     signal((beyond[0], col_of(other)))
     signal((mate[0], col_of(other)))
@@ -132,7 +128,7 @@
                     ].astype(ref.dtype)
 
     put(s0, adjoint(other))
-    met = n_xy - 1 + 8 + jnp.where(inland, 1, 0)
+    met = n_xy - 1 + 6 + jnp.where(inland, 1, 0)
     pl.semaphore_wait(barrier, met + 2 * zh)
     signal(zpart)
     signal(zpair)
@@ -331,23 +327,13 @@
         def _():
             give(r).start()
 
-        @pl.when(q != half)
-        def _():
-            far(r).start()
-
     def near(r):
         return remote(
             hs.at[half, r, 1 - a], r2.at[core], h_s.at[r], h_r.at[core], (mate[0], col_of(r))
         )
 
-    def far(r):
-        return remote(
-            hs.at[1 - half, r, 1], rd.at[core, a], fa_s.at[r], fa_r.at[core],
-            ((1 - half) * n_j + 2 + b, col_of(r)),
-        )
-
     def give(r):
-        return remote(hs.at[1 - half, r, 0], rg.at[r], g_s.at[r], g_r.at[r], mate)
+        return remote(hs.at[1 - half, r, 1 - a], rg.at[r], g_s.at[r], g_r.at[r], mate)
 
     def across(r):
         return remote(l2s.at[r], rc.at[core], cr_s.at[r], cr_r.at[core], (beyond[0], col_of(r)))
@@ -355,19 +341,22 @@
     def local():
         return remote(hs.at[half, other, a], rl, lo_s, lo_r, sib)
 
-    def cross():
-        for r in order_of_rows:
+    def cross(giving):
+        for r in (core, other):
             give(r).wait_recv()
-            l2s[r] = (hs[1 - half, r, 0].astype(F32) + rg[r].astype(F32)).astype(BF16)
+            l2s[r] = (hs[1 - half, r, a].astype(F32) + rg[r].astype(F32)).astype(BF16)
             across(r).start()
+            if giving:
+                give(r).start()
 
     for q in batches:
         remote(r1.at[q, span], r1.at[q, span], ag_s.at[q], ag_r.at[q], sib).wait_recv()
         if q == 0:
             swap(core).wait_recv()
+        forward(core, q)
+        if q == 0:
             swap(other).wait_recv()
-        for r in order_of_rows:
-            forward(r, q)
+        forward(other, q)
 
         @pl.when(q == half)
         def _():
@@ -375,7 +364,11 @@
 
         @pl.when((q != half) & (a == 0))
         def _():
-            cross()
+            cross(True)
+
+    @pl.when(a == 1)
+    def _():
+        cross(False)
 
     for f in (core, other):
         if f is core:
@@ -385,18 +378,8 @@
             total = rl[...].astype(F32)
         remote(r2.at[f], r2.at[f], h_s.at[f], h_r.at[f], sib).wait_recv()
         total = total + r2[f].astype(F32)
-
-        @pl.when(a == 0)
-        def _():
-            remote(rc.at[f], rc.at[f], cr_s.at[f], cr_r.at[f], sib).wait_recv()
-            xs[...] = rc[f].astype(F32)
-
-        @pl.when(a == 1)
-        def _():
-            remote(rd.at[f], rd.at[f], fa_s.at[f], fa_r.at[f], sib).wait_recv()
-            xs[...] = rd[f, 0].astype(F32) + rd[f, 1].astype(F32)
-
-        total = total + xs[...]
+        remote(rc.at[f], rc.at[f], cr_s.at[f], cr_r.at[f], sib).wait_recv()
+        total = total + rc[f].astype(F32)
         level = nv_ref[pl.ds(f, 1), :]
         for c in range(2):
             first = pl.multiple_of(f * 512 + c * 256 + half * 128 + a * 64, 64)
@@ -423,16 +406,8 @@
         remote(r1.at[q, span], r1.at[q, span], ag_s.at[q], ag_r.at[q], sib).wait_send()
         swap(q).wait_send()
         near(q).wait_send()
-        far(q).wait_send()
-
-        @pl.when(a == 1)
-        def _():
-            give(q).wait_send()
-
-        @pl.when(a == 0)
-        def _():
-            across(q).wait_send()
-
+        give(q).wait_send()
+        across(q).wait_send()
     core_swap.wait_send()
     local().wait_send()
 
@@ -477,13 +452,11 @@
             pltpu.VMEM((2, 2 * pw, 256), BF16),
             pltpu.VMEM((2, 2 * pw, 256), BF16),
             pltpu.VMEM((2, 2 * pw, 256), BF16),
-            pltpu.VMEM((2, 2, 2 * pw, 256), BF16),
-            pltpu.VMEM((2 * pw, 256), F32),
             pltpu.VMEM((2 * pw, 256), BF16),
             dma((4,)), dma((4,)), dma((4,)), dma((2,)), dma((2,)), dma((2,)), dma((2,)), dma((2,)),
             dma((2,)), dma((2,)), dma((2,)), dma, dma,
             dma((2,)), dma((2,)), dma((2,)), dma((2,)), dma((2,)), dma((2,)), dma((2,)), dma((2,)),
-            dma((2,)), dma((2,)), dma, dma,
+            dma, dma,
         ],
         compiler_params=pltpu.CompilerParams(
             collective_id=0, has_side_effects=True, vmem_limit_bytes=60 * 1024 * 1024

time: 61.6 us -> 61.4 us (level)
  the two profiles are of different devices: /device:TPU:8 before, /device:TPU:143 now
where the time goes in v5:
time: 61.4 us; the launch traced here: 61.2 us
  Pallas kernels  59.6 us (97%)
  local copies, waits for them, and re-layouts  1.66 us (3%)
    pallas_call x1, Pallas kernels, shards(): pl.pallas_call(functools.partial(body, n_row, n_col), out_shape=jax.Shape...  59.6 us
    reshape x1, local copies, waits for them, and re-layouts, shards(): return jnp.transpose(out.reshape(2, 2, pw, 256), (2, 0, 1, 3))  1.66 us

profile of v5, /device:TPU:143, one launch (start us, length us, event | category | flops | bytes accessed | tf_op | source)
XLA Modules:
  0.0 61.2 jit_solution(17673925796891660126)
XLA Ops:
  0.0 59.6 %shard_map.46 = f32[128,256]{1,0:T(8,128)} custom-call(bf16[1024,256]{1,0:T(8,128)(2,1)} %bitcast.6, bf16[256,2,2,256]{3,2,1,0:T(2,128)(2,1)} %v_hbm.1, f32[2,256]{1,0:T(2,128)} %nv_hbm.1, f32[1,256]{1,0:T(1,128)} %bitcast.8), custom_call_target="tpu_custom_call" | custom-call | tf_op jit(solution)/shard_map/pallas_call | solution.py:425
  59.6 1.7 %copy.7 = f32[2,2,32,256]{3,1,0,2:T(2,128)} copy(f32[2,2,32,256]{3,2,1,0:T(8,128)} %bitcast.7) | data formatting | bytes 262144 | tf_op jit(solution)/shard_map/reshape | solution.py:465
